TPU v7x, 32 devices: a whole 2x2x4 slice. The times are simulated.
32 devices in a mesh: tx: 4 (over x, core), ty: 8 (over z, y).
Axes of the slice: x: 2, y: 2, z: 4, core: 2. Of those that a mesh axis runs over, the one named last changes fastest.
Arguments:
- prior_state: float32 [2, 32, 256, 256], P(None, 'tx', 'ty'), may hold values from -6 to 6
- east_vel: float32 [2, 32, 256], P(None, 'tx', 'ty'), may hold values from -0.4 to 0.4
- north_vel: float32 [2, 32, 256], P(None, 'tx', 'ty'), may hold values from -0.4 to 0.4
- owner_tiles: int32 [3, 8], replicated, may hold values from 0 to 31, as said below
- obs_cells: int32 [3, 8, 128], replicated, may hold values from 0 to 511
- obs_value: float32 [3, 8, 128], replicated, may hold values from -6 to 6
- obs_error: float32 [3, 8, 128], replicated, may hold values from 0.1 to 1
- obs_pert: float32 [3, 8, 128, 256], replicated, may hold values from -6 to 6
Outputs:
- analysis: float32 [2, 32, 256, 256], P(None, 'tx', 'ty')
Inputs may be any that keep to these rules, and one draw needn't show every extreme that they name: `owner_tiles`: the 8 owners of one section hold distinct tiles.
All inputs are finite; a program needn't handle non-finite values.
Results may differ from a plain program's by a relative error of at most 0.0001.
Values sent between devices are 32-bit elements; how exact they have to be, the bound alone decides.
A program may use at most 128 MiB of HBM per device.

v0:
```python
import jax
import jax.numpy as jnp
from jax import lax
from jax.sharding import PartitionSpec as P

NU_COEF = 0.2
DAMP_COEF = 0.3
VERT_COEF = 0.6


def padded_2(cells, sides, width):
    for axis, dim in sides:
        count = lax.axis_size(axis)
        ends = count - 1
        head = lax.slice_in_dim(cells, 0, width, axis=dim)
        tail = lax.slice_in_dim(cells, cells.shape[dim] - width, cells.shape[dim], axis=dim)
        cells = jnp.concatenate(
            [
                lax.ppermute(tail, axis, [(i, (i + 1) % count) for i in range(ends)]),
                cells,
                lax.ppermute(head, axis, [((i + 1) % count, i) for i in range(ends)]),
            ],
            axis=dim,
        )
    return cells


def passed_along(array, axis, by):
    devices = lax.axis_size(axis)
    pairs = [(i, i + by) for i in range(devices) if 0 <= i + by < devices]
    return lax.ppermute(array, axis, pairs)


def advance(prior_state, east_vel, north_vel):
    padded = padded_2(prior_state, (("tx", 1), ("ty", 2)), 1)
    east_cells = padded[:, 2:, 1:-1]
    west_cells = padded[:, :-2, 1:-1]
    north_cells = padded[:, 1:-1, 2:]
    south_cells = padded[:, 1:-1, :-2]
    east_speed = east_vel[..., None]
    north_speed = north_vel[..., None]
    return (
        prior_state
        + NU_COEF * (east_cells + west_cells + north_cells + south_cells - 4.0 * prior_state)
        - 0.5 * east_speed * (east_cells - west_cells)
        - 0.5 * north_speed * (north_cells - south_cells)
        - DAMP_COEF * jnp.tanh(prior_state)
    )


def ramp(distance, radius):
    return jnp.square(jnp.maximum(0.0, 1.0 - jnp.abs(distance) / radius))


def taper(start_x, count_x, start_y, count_y, obs_x, obs_y, obs_level, levels, radius_x, radius_y):
    cell_x = start_x + jnp.arange(count_x, dtype=jnp.int32)
    cell_y = start_y + jnp.arange(count_y, dtype=jnp.int32)
    weight_x = ramp((cell_x[:, None] - obs_x[None, :]).astype(jnp.float32), radius_x)
    weight_y = ramp((cell_y[:, None] - obs_y[None, :]).astype(jnp.float32), radius_y)
    same_level = jnp.arange(levels, dtype=jnp.int32)[:, None] == obs_level[None, :]
    weight_l = jnp.where(same_level, jnp.float32(1.0), jnp.float32(VERT_COEF))
    joined = weight_l[:, None, None, :] * weight_x[None, :, None, :] * weight_y[None, None, :, :]
    return joined.reshape(levels * count_x * count_y, obs_x.shape[0])


def positions(tile_id, obs_cell, size_x, size_y, tiles_y):
    tile_i = tile_id // tiles_y
    tile_j = tile_id % tiles_y
    obs_level = obs_cell // (size_x * size_y)
    remain = obs_cell % (size_x * size_y)
    obs_x = tile_i * size_x + remain // size_y
    obs_y = tile_j * size_y + remain % size_y
    return (obs_level, obs_x, obs_y)


def prepare(prior_obs, values, errors, obs_noise, members):
    ens_mean = jnp.mean(prior_obs, axis=1, keepdims=True)
    anomaly = prior_obs - ens_mean
    spread = jnp.sum(anomaly * anomaly, axis=1) / (members - 1)
    factor = 1.0 / ((members - 1) * (spread + errors))
    innovation = values[:, None] + jnp.sqrt(errors)[:, None] * obs_noise - prior_obs
    return (anomaly, innovation, factor)


def update(state_anom, anomaly, innovation, factor, weights_taper):
    covar = jnp.dot(
        state_anom, anomaly.T, precision=lax.Precision.HIGHEST, preferred_element_type=jnp.float32
    )
    weights = covar * weights_taper * factor[None, :]
    return jnp.dot(
        weights, innovation, precision=lax.Precision.HIGHEST, preferred_element_type=jnp.float32
    )


def spread_east_first(payload):
    first_list = []
    for offset in range(7):
        if offset == 3:
            first_list.append(payload)
        else:
            first_list.append(passed_along(payload, "tx", 3 - offset))
    first_stack = jnp.stack(first_list)
    second_list = []
    for offset in range(7):
        if offset == 3:
            second_list.append(first_stack)
        else:
            second_list.append(passed_along(first_stack, "ty", 3 - offset))
    return jnp.stack(second_list, axis=1)


def on_device(
    prior_state, east_vel, north_vel, owner_tiles, obs_cells, obs_value, obs_error, obs_pert
):
    levels, size_x, size_y, members = prior_state.shape
    section_count, owner_count = owner_tiles.shape
    tiles_y = lax.axis_size("ty")
    column_idx = lax.axis_index("tx")
    row_idx = lax.axis_index("ty")
    my_tile = column_idx * tiles_y + row_idx
    model_state = advance(prior_state, east_vel, north_vel)
    for section_num in range(section_count):
        flat_state = model_state.reshape(levels * size_x * size_y, members)
        state_anom = flat_state - jnp.mean(flat_state, axis=1, keepdims=True)
        payload = jnp.zeros((obs_cells.shape[2], members), jnp.float32)
        for owner_num in range(owner_count):
            mine = owner_tiles[section_num, owner_num] == my_tile
            payload = payload + jnp.where(mine, flat_state[obs_cells[section_num, owner_num]], 0.0)
        neighbourhood = spread_east_first(payload)
        total_inc = jnp.zeros(flat_state.shape, jnp.float32)
        for owner_num in range(owner_count):
            tile_id = owner_tiles[section_num, owner_num]
            step_x = tile_id // tiles_y - column_idx
            step_y = tile_id % tiles_y - row_idx
            slot_x = jnp.clip(step_x + 3, 0, 6)
            slot_y = jnp.clip(step_y + 3, 0, 6)
            arrived = neighbourhood[slot_x, slot_y]
            anomaly, innovation, factor = prepare(
                arrived,
                obs_value[section_num, owner_num],
                obs_error[section_num, owner_num],
                obs_pert[section_num, owner_num],
                members,
            )
            obs_level, obs_x, obs_y = positions(
                tile_id, obs_cells[section_num, owner_num], size_x, size_y, tiles_y
            )
            weights_taper = taper(
                column_idx * size_x,
                size_x,
                row_idx * size_y,
                size_y,
                obs_x,
                obs_y,
                obs_level,
                levels,
                3.0 * size_x,
                3.0 * size_y,
            )
            increment = update(state_anom, anomaly, innovation, factor, weights_taper)
            total_inc = total_inc + increment
        model_state = model_state + total_inc.reshape(levels, size_x, size_y, members)
    return model_state


def solution(mesh):
    placed = (
        P(None, "tx", "ty", None),
        P(None, "tx", "ty"),
        P(None, "tx", "ty"),
        P(),
        P(),
        P(),
        P(),
        P(),
    )
    return jax.shard_map(
        on_device, mesh=mesh, in_specs=placed, out_specs=P(None, "tx", "ty", None), check_vma=False
    )
```

profile of v0, /device:TPU:4, one launch (start us, length us, event | category | flops | bytes accessed | tf_op | source)
XLA Modules:
  0.0 547.7 jit_solution(9515680152225035523)
XLA Ops:
  0.9 1.7 collective-permute-start.1
  4.0 2.1 fusion.536
  7.6 1.6 fusion.451
  73.2 1.7 bitcast_sqrt_fusion
  74.8 1.7 slice_bitcast_fusion
  97.1 1.9 collective-permute-start.2
  99.0 4.8 collective-permute-start.3
  110.0 2.3 fusion.533
  122.0 3.7 collective-permute-start.4
  133.3 2.8 collective-permute-start.5
  142.4 4.7 collective-permute-done.8
  148.7 3.7 collective-permute-start.10
  153.6 3.4 collective-permute-start.11
  158.5 2.8 collective-permute-start.12
  162.1 3.1 collective-permute-start.13
  166.5 6.6 %collective-permute-done.10 = f32[7,128,256]{2,1,0:T(8,128)S(1)} collective-permute-done((f32[7,128,256]{2,1,0:T(8,128)S(1)}, f32[7,128,256]{2,1,0:T(8,128)S(1)}, u32[]{:S(2)}, u32[]{:S(2)}) %collective-permute-start.10) | collective-permute-done | bytes 917536 | tf_op jit(solution)/shard_map/ppermute | solution.py:31
  174.7 18.1 %collective-permute-done.11 = f32[7,128,256]{2,1,0:T(8,128)S(1)} collective-permute-done((f32[7,128,256]{2,1,0:T(8,128)S(1)}, f32[7,128,256]{2,1,0:T(8,128)S(1)}, u32[]{:S(2)}, u32[]{:S(2)}) %collective-permute-start.11) | collective-permute-done | bytes 917536 | tf_op jit(solution)/shard_map/ppermute | solution.py:31
  192.9 30.9 %collective-permute-done.12 = f32[7,128,256]{2,1,0:T(8,128)S(1)} collective-permute-done((f32[7,128,256]{2,1,0:T(8,128)S(1)}, f32[7,128,256]{2,1,0:T(8,128)S(1)}, u32[]{:S(2)}, u32[]{:S(2)}) %collective-permute-start.12) | collective-permute-done | bytes 917536 | tf_op jit(solution)/shard_map/ppermute | solution.py:31
  224.2 27.8 %collective-permute-done.15 = f32[7,128,256]{2,1,0:T(8,128)S(1)} collective-permute-done((f32[7,128,256]{2,1,0:T(8,128)S(1)}, f32[7,128,256]{2,1,0:T(8,128)S(1)}, u32[]{:S(2)}, u32[]{:S(2)}) %collective-permute-start.15) | collective-permute-done | bytes 917536 | tf_op jit(solution)/shard_map/ppermute | solution.py:31
  265.8 1.6 convolution_add_fusion.17
  268.9 1.6 convolution_add_fusion.15
  270.5 1.6 convolution_add_fusion.14
  283.0 2.7 collective-permute-start.16
  293.5 2.0 collective-permute-start.18
  300.5 4.7 collective-permute-done.20
  311.6 2.5 collective-permute-start.24
  315.0 3.3 collective-permute-start.25
  319.6 9.3 %collective-permute-done.22 = f32[7,128,256]{2,1,0:T(8,128)S(1)} collective-permute-done((f32[7,128,256]{2,1,0:T(8,128)S(1)}, f32[7,128,256]{2,1,0:T(8,128)S(1)}, u32[]{:S(2)}, u32[]{:S(2)}) %collective-permute-start.22) | collective-permute-done | bytes 917536 | tf_op jit(solution)/shard_map/ppermute | solution.py:31
  330.3 18.3 %collective-permute-done.23 = f32[7,128,256]{2,1,0:T(8,128)S(1)} collective-permute-done((f32[7,128,256]{2,1,0:T(8,128)S(1)}, f32[7,128,256]{2,1,0:T(8,128)S(1)}, u32[]{:S(2)}, u32[]{:S(2)}) %collective-permute-start.23) | collective-permute-done | bytes 917536 | tf_op jit(solution)/shard_map/ppermute | solution.py:31
  348.6 27.8 %collective-permute-done.24 = f32[7,128,256]{2,1,0:T(8,128)S(1)} collective-permute-done((f32[7,128,256]{2,1,0:T(8,128)S(1)}, f32[7,128,256]{2,1,0:T(8,128)S(1)}, u32[]{:S(2)}, u32[]{:S(2)}) %collective-permute-start.24) | collective-permute-done | bytes 917536 | tf_op jit(solution)/shard_map/ppermute | solution.py:31
  376.9 19.9 %collective-permute-done.27 = f32[7,128,256]{2,1,0:T(8,128)S(1)} collective-permute-done((f32[7,128,256]{2,1,0:T(8,128)S(1)}, f32[7,128,256]{2,1,0:T(8,128)S(1)}, u32[]{:S(2)}, u32[]{:S(2)}) %collective-permute-start.27) | collective-permute-done | bytes 917536 | tf_op jit(solution)/shard_map/ppermute | solution.py:31
  406.4 1.6 convolution_add_fusion.12
  408.0 1.6 convolution_add_fusion.11
  411.2 1.6 convolution_add_fusion.9
  412.8 1.6 convolution_add_fusion.8
  414.4 1.6 convolution_add_fusion.7
  422.9 2.1 collective-permute-start.28
  426.4 2.0 collective-permute-start.30
  432.5 5.4 collective-permute-done.32
  439.4 1.8 collective-permute-start.34
  442.7 3.0 collective-permute-start.36
  445.8 2.9 collective-permute-start.37
  450.0 12.0 %collective-permute-done.34 = f32[7,128,256]{2,1,0:T(8,128)S(1)} collective-permute-done((f32[7,128,256]{2,1,0:T(8,128)S(1)}, f32[7,128,256]{2,1,0:T(8,128)S(1)}, u32[]{:S(2)}, u32[]{:S(2)}) %collective-permute-start.34) | collective-permute-done | bytes 917536 | tf_op jit(solution)/shard_map/ppermute | solution.py:31
  463.4 18.3 %collective-permute-done.35 = f32[7,128,256]{2,1,0:T(8,128)S(1)} collective-permute-done((f32[7,128,256]{2,1,0:T(8,128)S(1)}, f32[7,128,256]{2,1,0:T(8,128)S(1)}, u32[]{:S(2)}, u32[]{:S(2)}) %collective-permute-start.35) | collective-permute-done | bytes 917536 | tf_op jit(solution)/shard_map/ppermute | solution.py:31
  481.8 25.5 %collective-permute-done.36 = f32[7,128,256]{2,1,0:T(8,128)S(1)} collective-permute-done((f32[7,128,256]{2,1,0:T(8,128)S(1)}, f32[7,128,256]{2,1,0:T(8,128)S(1)}, u32[]{:S(2)}, u32[]{:S(2)}) %collective-permute-start.36) | collective-permute-done | bytes 917536 | tf_op jit(solution)/shard_map/ppermute | solution.py:31
  507.7 20.0 %collective-permute-done.39 = f32[7,128,256]{2,1,0:T(8,128)S(1)} collective-permute-done((f32[7,128,256]{2,1,0:T(8,128)S(1)}, f32[7,128,256]{2,1,0:T(8,128)S(1)}, u32[]{:S(2)}, u32[]{:S(2)}) %collective-permute-start.39) | collective-permute-done | bytes 917536 | tf_op jit(solution)/shard_map/ppermute | solution.py:31
  534.0 1.6 fusion.75
  541.9 1.6 convolution_add_fusion.2
  (451 shorter events, 144.3 us)
Async XLA Ops:
  0.0 96.1 %copy-start = (f32[2,8,32,256]{3,2,1,0:T(8,128)S(1)}, f32[2,8,32,256]{3,2,1,0:T(8,128)}, u32[]{:S(2)}) copy-start(f32[2,8,32,256]{3,2,1,0:T(8,128)} %param.8) | copy-start | bytes 1572868
  0.9 95.2 %collective-permute-start.1 = (f32[2,1,32,256]{3,2,1,0:T(8,128)S(1)}, f32[2,1,32,256]{3,2,1,0:T(8,128)S(1)}, u32[]{:S(2)}, u32[]{:S(2)}) collective-permute-start(f32[2,1,32,256]{3,2,1,0:T(8,128)S(1)} %get-tuple-element.158), channel_id=1, source_target_pairs={{0,8},{8,16},{16,24},{1,9},{9,17},{17,25},{2,10},{10,18},{18,26},{... | collective-permute-start | bytes 196616 | tf_op jit(solution)/shard_map/ppermute | solution.py:19
  2.7 93.5 %collective-permute-start = (f32[2,1,32,256]{3,2,1,0:T(8,128)S(1)}, f32[2,1,32,256]{3,2,1,0:T(8,128)S(1)}, u32[]{:S(2)}, u32[]{:S(2)}) collective-permute-start(f32[2,1,32,256]{3,2,1,0:T(8,128)S(1)} %get-tuple-element.157), channel_id=1, source_target_pairs={{8,0},{16,8},{24,16},{9,1},{17,9},{25,17},{10,2},{18,10},{26,18},{... | collective-permute-start | bytes 196616 | tf_op jit(solution)/shard_map/ppermute | solution.py:21
  97.1 12.3 %collective-permute-start.2 = (f32[2,10,1,256]{3,2,1,0:T(1,128)S(1)}, f32[2,10,1,256]{3,2,1,0:T(1,128)S(1)}, u32[]{:S(2)}, u32[]{:S(2)}) collective-permute-start(f32[2,10,1,256]{3,2,1,0:T(1,128)S(1)} %get-tuple-element.155), channel_id=1, source_target_pairs={{1,0},{2,1},{3,2},{4,3},{5,4},{6,5},{7,6},{9,8},{10,9},{11,10},{12... | collective-permute-start | bytes 61448 | tf_op jit(solution)/shard_map/ppermute | solution.py:21
  99.0 10.4 %collective-permute-start.3 = (f32[2,10,1,256]{3,2,1,0:T(1,128)S(1)}, f32[2,10,1,256]{3,2,1,0:T(1,128)S(1)}, u32[]{:S(2)}, u32[]{:S(2)}) collective-permute-start(f32[2,10,1,256]{3,2,1,0:T(1,128)S(1)} %get-tuple-element.156), channel_id=1, source_target_pairs={{0,1},{1,2},{2,3},{3,4},{4,5},{5,6},{6,7},{8,9},{9,10},{10,11},{11... | collective-permute-start | bytes 61448 | tf_op jit(solution)/shard_map/ppermute | solution.py:19
  122.0 18.1 %collective-permute-start.4 = (f32[128,256]{1,0:T(8,128)}, f32[128,256]{1,0:T(8,128)S(1)}, u32[]{:S(2)}, u32[]{:S(2)}) collective-permute-start(f32[128,256]{1,0:T(8,128)} %select_add_fusion.2), channel_id=1, source_target_pairs={{0,24},{1,25},{2,26},{3,27},{4,28},{5,29},{6,30},{7,31}} | collective-permute-start | bytes 393224 | tf_op jit(solution)/shard_map/ppermute | solution.py:31
  133.3 8.1 %collective-permute-start.5 = (f32[128,256]{1,0:T(8,128)}, f32[128,256]{1,0:T(8,128)S(1)}, u32[]{:S(2)}, u32[]{:S(2)}) collective-permute-start(f32[128,256]{1,0:T(8,128)} %select_add_fusion.2), channel_id=1, source_target_pairs={{0,16},{8,24},{1,17},{9,25},{2,18},{10,26},{3,19},{11,27},{4,20},{... | collective-permute-start | bytes 393224 | tf_op jit(solution)/shard_map/ppermute | solution.py:31
  136.2 5.3 collective-permute-start.6
  137.5 4.9 collective-permute-start.7
  138.8 8.3 %collective-permute-start.8 = (f32[128,256]{1,0:T(8,128)}, f32[128,256]{1,0:T(8,128)S(1)}, u32[]{:S(2)}, u32[]{:S(2)}) collective-permute-start(f32[128,256]{1,0:T(8,128)} %select_add_fusion.2), channel_id=1, source_target_pairs={{16,0},{24,8},{17,1},{25,9},{18,2},{26,10},{19,3},{27,11},{20,4},{... | collective-permute-start | bytes 393224 | tf_op jit(solution)/shard_map/ppermute | solution.py:31
  140.1 8.6 %collective-permute-start.9 = (f32[128,256]{1,0:T(8,128)}, f32[128,256]{1,0:T(8,128)S(1)}, u32[]{:S(2)}, u32[]{:S(2)}) collective-permute-start(f32[128,256]{1,0:T(8,128)} %select_add_fusion.2), channel_id=1, source_target_pairs={{24,0},{25,1},{26,2},{27,3},{28,4},{29,5},{30,6},{31,7}} | collective-permute-start | bytes 393224 | tf_op jit(solution)/shard_map/ppermute | solution.py:31
  148.7 24.5 %collective-permute-start.10 = (f32[7,128,256]{2,1,0:T(8,128)S(1)}, f32[7,128,256]{2,1,0:T(8,128)S(1)}, u32[]{:S(2)}, u32[]{:S(2)}) collective-permute-start(f32[7,128,256]{2,1,0:T(8,128)S(1)} %bitcast_dynamic-update-slice_fusion.35), channel_id=1, source_target_pairs={{0,3},{1,4},{2,5},{3,6},{4,7},{8,11},{9,12},{10,13},{11,14},{12,15... | collective-permute-start | bytes 2752520 | tf_op jit(solution)/shard_map/ppermute | solution.py:31
  153.6 39.2 %collective-permute-start.11 = (f32[7,128,256]{2,1,0:T(8,128)S(1)}, f32[7,128,256]{2,1,0:T(8,128)S(1)}, u32[]{:S(2)}, u32[]{:S(2)}) collective-permute-start(f32[7,128,256]{2,1,0:T(8,128)S(1)} %bitcast_dynamic-update-slice_fusion.35), channel_id=1, source_target_pairs={{0,2},{1,3},{2,4},{3,5},{4,6},{5,7},{8,10},{9,11},{10,12},{11,13},... | collective-permute-start | bytes 2752520 | tf_op jit(solution)/shard_map/ppermute | solution.py:31
  158.5 65.3 %collective-permute-start.12 = (f32[7,128,256]{2,1,0:T(8,128)S(1)}, f32[7,128,256]{2,1,0:T(8,128)S(1)}, u32[]{:S(2)}, u32[]{:S(2)}) collective-permute-start(f32[7,128,256]{2,1,0:T(8,128)S(1)} %bitcast_dynamic-update-slice_fusion.35), channel_id=1, source_target_pairs={{0,1},{1,2},{2,3},{3,4},{4,5},{5,6},{6,7},{8,9},{9,10},{10,11},{11... | collective-permute-start | bytes 2752520 | tf_op jit(solution)/shard_map/ppermute | solution.py:31
  162.1 61.9 %collective-permute-start.13 = (f32[7,128,256]{2,1,0:T(8,128)S(1)}, f32[7,128,256]{2,1,0:T(8,128)S(1)}, u32[]{:S(2)}, u32[]{:S(2)}) collective-permute-start(f32[7,128,256]{2,1,0:T(8,128)S(1)} %bitcast_dynamic-update-slice_fusion.35), channel_id=1, source_target_pairs={{1,0},{2,1},{3,2},{4,3},{5,4},{6,5},{7,6},{9,8},{10,9},{11,10},{12... | collective-permute-start | bytes 2752520 | tf_op jit(solution)/shard_map/ppermute | solution.py:31
  165.2 58.9 %collective-permute-start.14 = (f32[7,128,256]{2,1,0:T(8,128)S(1)}, f32[7,128,256]{2,1,0:T(8,128)S(1)}, u32[]{:S(2)}, u32[]{:S(2)}) collective-permute-start(f32[7,128,256]{2,1,0:T(8,128)S(1)} %bitcast_dynamic-update-slice_fusion.35), channel_id=1, source_target_pairs={{2,0},{3,1},{4,2},{5,3},{6,4},{7,5},{10,8},{11,9},{12,10},{13,11},... | collective-permute-start | bytes 2752520 | tf_op jit(solution)/shard_map/ppermute | solution.py:31
  173.1 78.9 %collective-permute-start.15 = (f32[7,128,256]{2,1,0:T(8,128)S(1)}, f32[7,128,256]{2,1,0:T(8,128)S(1)}, u32[]{:S(2)}, u32[]{:S(2)}) collective-permute-start(f32[7,128,256]{2,1,0:T(8,128)S(1)} %bitcast_dynamic-update-slice_fusion.35), channel_id=1, source_target_pairs={{3,0},{4,1},{5,2},{6,3},{7,4},{11,8},{12,9},{13,10},{14,11},{15,12... | collective-permute-start | bytes 2752520 | tf_op jit(solution)/shard_map/ppermute | solution.py:31
  174.7 79.2 %copy-start.5 = (f32[2,8,32,128]{3,2,1,0:T(8,128)S(1)}, f32[2,8,32,128]{3,2,1,0:T(8,128)}, u32[]{:S(2)}) copy-start(f32[2,8,32,128]{3,2,1,0:T(8,128)} %broadcast_multiply_fusion.16) | copy-start | bytes 786436
  192.9 61.8 %copy-start.6 = (f32[2,8,32,128]{3,2,1,0:T(8,128)S(1)}, f32[2,8,32,128]{3,2,1,0:T(8,128)}, u32[]{:S(2)}) copy-start(f32[2,8,32,128]{3,2,1,0:T(8,128)} %broadcast_multiply_fusion.17) | copy-start | bytes 786436
  192.9 62.4 %copy-start.7 = (f32[2,8,32,128]{3,2,1,0:T(8,128)S(1)}, f32[2,8,32,128]{3,2,1,0:T(8,128)}, u32[]{:S(2)}) copy-start(f32[2,8,32,128]{3,2,1,0:T(8,128)} %broadcast_multiply_fusion.18) | copy-start | bytes 786436
  224.1 34.0 %copy-start.11 = (f32[2,8,32,128]{3,2,1,0:T(8,128)S(1)}, f32[2,8,32,128]{3,2,1,0:T(8,128)}, u32[]{:S(2)}) copy-start(f32[2,8,32,128]{3,2,1,0:T(8,128)} %broadcast_multiply_fusion.22) | copy-start | bytes 786436
  224.2 34.6 %copy-start.12 = (f32[2,8,32,128]{3,2,1,0:T(8,128)S(1)}, f32[2,8,32,128]{3,2,1,0:T(8,128)}, u32[]{:S(2)}) copy-start(f32[2,8,32,128]{3,2,1,0:T(8,128)} %broadcast_multiply_fusion.23) | copy-start | bytes 786436
  224.2 35.2 %copy-start.59 = (f32[128]{0:T(128)S(1)}, f32[128]{0:T(128)}, u32[]{:S(2)}) copy-start(f32[128]{0:T(128)} %get-tuple-element.179) | copy-start | bytes 1540
  283.0 15.2 %collective-permute-start.16 = (f32[128,256]{1,0:T(8,128)}, f32[128,256]{1,0:T(8,128)S(1)}, u32[]{:S(2)}, u32[]{:S(2)}) collective-permute-start(f32[128,256]{1,0:T(8,128)} %select_add_fusion.1), channel_id=1, source_target_pairs={{0,24},{1,25},{2,26},{3,27},{4,28},{5,29},{6,30},{7,31}} | collective-permute-start | bytes 393224 | tf_op jit(solution)/shard_map/ppermute | solution.py:31
  292.2 7.3 %collective-permute-start.17 = (f32[128,256]{1,0:T(8,128)}, f32[128,256]{1,0:T(8,128)S(1)}, u32[]{:S(2)}, u32[]{:S(2)}) collective-permute-start(f32[128,256]{1,0:T(8,128)} %select_add_fusion.1), channel_id=1, source_target_pairs={{0,16},{8,24},{1,17},{9,25},{2,18},{10,26},{3,19},{11,27},{4,20},{... | collective-permute-start | bytes 393224 | tf_op jit(solution)/shard_map/ppermute | solution.py:31
  293.5 6.0 %collective-permute-start.18 = (f32[128,256]{1,0:T(8,128)}, f32[128,256]{1,0:T(8,128)S(1)}, u32[]{:S(2)}, u32[]{:S(2)}) collective-permute-start(f32[128,256]{1,0:T(8,128)} %select_add_fusion.1), channel_id=1, source_target_pairs={{0,8},{8,16},{16,24},{1,9},{9,17},{17,25},{2,10},{10,18},{18,26},{... | collective-permute-start | bytes 393224 | tf_op jit(solution)/shard_map/ppermute | solution.py:31
  295.6 4.9 collective-permute-start.19
  296.9 8.3 %collective-permute-start.20 = (f32[128,256]{1,0:T(8,128)}, f32[128,256]{1,0:T(8,128)S(1)}, u32[]{:S(2)}, u32[]{:S(2)}) collective-permute-start(f32[128,256]{1,0:T(8,128)} %select_add_fusion.1), channel_id=1, source_target_pairs={{16,0},{24,8},{17,1},{25,9},{18,2},{26,10},{19,3},{27,11},{20,4},{... | collective-permute-start | bytes 393224 | tf_op jit(solution)/shard_map/ppermute | solution.py:31
  298.2 8.6 %collective-permute-start.21 = (f32[128,256]{1,0:T(8,128)}, f32[128,256]{1,0:T(8,128)S(1)}, u32[]{:S(2)}, u32[]{:S(2)}) collective-permute-start(f32[128,256]{1,0:T(8,128)} %select_add_fusion.1), channel_id=1, source_target_pairs={{24,0},{25,1},{26,2},{27,3},{28,4},{29,5},{30,6},{31,7}} | collective-permute-start | bytes 393224 | tf_op jit(solution)/shard_map/ppermute | solution.py:31
  306.8 22.1 %collective-permute-start.22 = (f32[7,128,256]{2,1,0:T(8,128)S(1)}, f32[7,128,256]{2,1,0:T(8,128)S(1)}, u32[]{:S(2)}, u32[]{:S(2)}) collective-permute-start(f32[7,128,256]{2,1,0:T(8,128)S(1)} %bitcast_dynamic-update-slice_fusion.28), channel_id=1, source_target_pairs={{0,3},{1,4},{2,5},{3,6},{4,7},{8,11},{9,12},{10,13},{11,14},{12,15... | collective-permute-start | bytes 2752520 | tf_op jit(solution)/shard_map/ppermute | solution.py:31
  309.6 39.0 %collective-permute-start.23 = (f32[7,128,256]{2,1,0:T(8,128)S(1)}, f32[7,128,256]{2,1,0:T(8,128)S(1)}, u32[]{:S(2)}, u32[]{:S(2)}) collective-permute-start(f32[7,128,256]{2,1,0:T(8,128)S(1)} %bitcast_dynamic-update-slice_fusion.28), channel_id=1, source_target_pairs={{0,2},{1,3},{2,4},{3,5},{4,6},{5,7},{8,10},{9,11},{10,12},{11,13},... | collective-permute-start | bytes 2752520 | tf_op jit(solution)/shard_map/ppermute | solution.py:31
  311.6 64.8 %collective-permute-start.24 = (f32[7,128,256]{2,1,0:T(8,128)S(1)}, f32[7,128,256]{2,1,0:T(8,128)S(1)}, u32[]{:S(2)}, u32[]{:S(2)}) collective-permute-start(f32[7,128,256]{2,1,0:T(8,128)S(1)} %bitcast_dynamic-update-slice_fusion.28), channel_id=1, source_target_pairs={{0,1},{1,2},{2,3},{3,4},{4,5},{5,6},{6,7},{8,9},{9,10},{10,11},{11... | collective-permute-start | bytes 2752520 | tf_op jit(solution)/shard_map/ppermute | solution.py:31
  315.0 61.6 %collective-permute-start.25 = (f32[7,128,256]{2,1,0:T(8,128)S(1)}, f32[7,128,256]{2,1,0:T(8,128)S(1)}, u32[]{:S(2)}, u32[]{:S(2)}) collective-permute-start(f32[7,128,256]{2,1,0:T(8,128)S(1)} %bitcast_dynamic-update-slice_fusion.28), channel_id=1, source_target_pairs={{1,0},{2,1},{3,2},{4,3},{5,4},{6,5},{7,6},{9,8},{10,9},{11,10},{12... | collective-permute-start | bytes 2752520 | tf_op jit(solution)/shard_map/ppermute | solution.py:31
  318.3 58.4 %collective-permute-start.26 = (f32[7,128,256]{2,1,0:T(8,128)S(1)}, f32[7,128,256]{2,1,0:T(8,128)S(1)}, u32[]{:S(2)}, u32[]{:S(2)}) collective-permute-start(f32[7,128,256]{2,1,0:T(8,128)S(1)} %bitcast_dynamic-update-slice_fusion.28), channel_id=1, source_target_pairs={{2,0},{3,1},{4,2},{5,3},{6,4},{7,5},{10,8},{11,9},{12,10},{13,11},... | collective-permute-start | bytes 2752520 | tf_op jit(solution)/shard_map/ppermute | solution.py:31
  328.9 67.9 %collective-permute-start.27 = (f32[7,128,256]{2,1,0:T(8,128)S(1)}, f32[7,128,256]{2,1,0:T(8,128)S(1)}, u32[]{:S(2)}, u32[]{:S(2)}) collective-permute-start(f32[7,128,256]{2,1,0:T(8,128)S(1)} %bitcast_dynamic-update-slice_fusion.28), channel_id=1, source_target_pairs={{3,0},{4,1},{5,2},{6,3},{7,4},{11,8},{12,9},{13,10},{14,11},{15,12... | collective-permute-start | bytes 2752520 | tf_op jit(solution)/shard_map/ppermute | solution.py:31
  330.3 67.5 %copy-start.16 = (f32[3,8,128]{2,1,0:T(8,128)S(1)}, f32[3,8,128]{2,1,0:T(8,128)}, u32[]{:S(2)}) copy-start(f32[3,8,128]{2,1,0:T(8,128)} %param.14) | copy-start | bytes 36868
  422.9 8.1 %collective-permute-start.28 = (f32[128,256]{1,0:T(8,128)S(1)}, f32[128,256]{1,0:T(8,128)S(1)}, u32[]{:S(2)}, u32[]{:S(2)}) collective-permute-start(f32[128,256]{1,0:T(8,128)S(1)} %select_add_fusion), channel_id=1, source_target_pairs={{0,24},{1,25},{2,26},{3,27},{4,28},{5,29},{6,30},{7,31}} | collective-permute-start | bytes 393224 | tf_op jit(solution)/shard_map/ppermute | solution.py:31
  425.1 7.3 %collective-permute-start.29 = (f32[128,256]{1,0:T(8,128)S(1)}, f32[128,256]{1,0:T(8,128)S(1)}, u32[]{:S(2)}, u32[]{:S(2)}) collective-permute-start(f32[128,256]{1,0:T(8,128)S(1)} %select_add_fusion), channel_id=1, source_target_pairs={{0,16},{8,24},{1,17},{9,25},{2,18},{10,26},{3,19},{11,27},{4,20},{... | collective-permute-start | bytes 393224 | tf_op jit(solution)/shard_map/ppermute | solution.py:31
  426.4 6.0 %collective-permute-start.30 = (f32[128,256]{1,0:T(8,128)S(1)}, f32[128,256]{1,0:T(8,128)S(1)}, u32[]{:S(2)}, u32[]{:S(2)}) collective-permute-start(f32[128,256]{1,0:T(8,128)S(1)} %select_add_fusion), channel_id=1, source_target_pairs={{0,8},{8,16},{16,24},{1,9},{9,17},{17,25},{2,10},{10,18},{18,26},{... | collective-permute-start | bytes 393224 | tf_op jit(solution)/shard_map/ppermute | solution.py:31
  428.4 4.0 collective-permute-start.31
  429.7 8.1 %collective-permute-start.32 = (f32[128,256]{1,0:T(8,128)S(1)}, f32[128,256]{1,0:T(8,128)S(1)}, u32[]{:S(2)}, u32[]{:S(2)}) collective-permute-start(f32[128,256]{1,0:T(8,128)S(1)} %select_add_fusion), channel_id=1, source_target_pairs={{16,0},{24,8},{17,1},{25,9},{18,2},{26,10},{19,3},{27,11},{20,4},{... | collective-permute-start | bytes 393224 | tf_op jit(solution)/shard_map/ppermute | solution.py:31
  431.0 8.4 %collective-permute-start.33 = (f32[128,256]{1,0:T(8,128)S(1)}, f32[128,256]{1,0:T(8,128)S(1)}, u32[]{:S(2)}, u32[]{:S(2)}) collective-permute-start(f32[128,256]{1,0:T(8,128)S(1)} %select_add_fusion), channel_id=1, source_target_pairs={{24,0},{25,1},{26,2},{27,3},{28,4},{29,5},{30,6},{31,7}} | collective-permute-start | bytes 393224 | tf_op jit(solution)/shard_map/ppermute | solution.py:31
  439.4 22.6 %collective-permute-start.34 = (f32[7,128,256]{2,1,0:T(8,128)S(1)}, f32[7,128,256]{2,1,0:T(8,128)S(1)}, u32[]{:S(2)}, u32[]{:S(2)}) collective-permute-start(f32[7,128,256]{2,1,0:T(8,128)S(1)} %bitcast_dynamic-update-slice_fusion.21), channel_id=1, source_target_pairs={{0,3},{1,4},{2,5},{3,6},{4,7},{8,11},{9,12},{10,13},{11,14},{12,15... | collective-permute-start | bytes 2752520 | tf_op jit(solution)/shard_map/ppermute | solution.py:31
  441.3 40.4 %collective-permute-start.35 = (f32[7,128,256]{2,1,0:T(8,128)S(1)}, f32[7,128,256]{2,1,0:T(8,128)S(1)}, u32[]{:S(2)}, u32[]{:S(2)}) collective-permute-start(f32[7,128,256]{2,1,0:T(8,128)S(1)} %bitcast_dynamic-update-slice_fusion.21), channel_id=1, source_target_pairs={{0,2},{1,3},{2,4},{3,5},{4,6},{5,7},{8,10},{9,11},{10,12},{11,13},... | collective-permute-start | bytes 2752520 | tf_op jit(solution)/shard_map/ppermute | solution.py:31
  442.7 64.6 %collective-permute-start.36 = (f32[7,128,256]{2,1,0:T(8,128)S(1)}, f32[7,128,256]{2,1,0:T(8,128)S(1)}, u32[]{:S(2)}, u32[]{:S(2)}) collective-permute-start(f32[7,128,256]{2,1,0:T(8,128)S(1)} %bitcast_dynamic-update-slice_fusion.21), channel_id=1, source_target_pairs={{0,1},{1,2},{2,3},{3,4},{4,5},{5,6},{6,7},{8,9},{9,10},{10,11},{11... | collective-permute-start | bytes 2752520 | tf_op jit(solution)/shard_map/ppermute | solution.py:31
  445.8 61.6 %collective-permute-start.37 = (f32[7,128,256]{2,1,0:T(8,128)S(1)}, f32[7,128,256]{2,1,0:T(8,128)S(1)}, u32[]{:S(2)}, u32[]{:S(2)}) collective-permute-start(f32[7,128,256]{2,1,0:T(8,128)S(1)} %bitcast_dynamic-update-slice_fusion.21), channel_id=1, source_target_pairs={{1,0},{2,1},{3,2},{4,3},{5,4},{6,5},{7,6},{9,8},{10,9},{11,10},{12... | collective-permute-start | bytes 2752520 | tf_op jit(solution)/shard_map/ppermute | solution.py:31
  448.7 58.8 %collective-permute-start.38 = (f32[7,128,256]{2,1,0:T(8,128)S(1)}, f32[7,128,256]{2,1,0:T(8,128)S(1)}, u32[]{:S(2)}, u32[]{:S(2)}) collective-permute-start(f32[7,128,256]{2,1,0:T(8,128)S(1)} %bitcast_dynamic-update-slice_fusion.21), channel_id=1, source_target_pairs={{2,0},{3,1},{4,2},{5,3},{6,4},{7,5},{10,8},{11,9},{12,10},{13,11},... | collective-permute-start | bytes 2752520 | tf_op jit(solution)/shard_map/ppermute | solution.py:31
  462.0 65.6 %collective-permute-start.39 = (f32[7,128,256]{2,1,0:T(8,128)S(1)}, f32[7,128,256]{2,1,0:T(8,128)S(1)}, u32[]{:S(2)}, u32[]{:S(2)}) collective-permute-start(f32[7,128,256]{2,1,0:T(8,128)S(1)} %bitcast_dynamic-update-slice_fusion.21), channel_id=1, source_target_pairs={{3,0},{4,1},{5,2},{6,3},{7,4},{11,8},{12,9},{13,10},{14,11},{15,12... | collective-permute-start | bytes 2752520 | tf_op jit(solution)/shard_map/ppermute | solution.py:31
  (52 other events, 745.8 us)
where the time goes:
time: 557 us; the launch traced here: 548 us
  waiting for transfers between devices  254 us (46%)
  starting transfers between devices  79.2 us (14%)
  between operations  78.8 us (14%)
  matrix products  53.2 us (10%)
  other arithmetic  42.8 us (8%)
  local copies, waits for them, and re-layouts  39.7 us (7%)
    ppermute x36, waiting for transfers between devices, passed_along(): return lax.ppermute(array, axis, pairs)  254 us
    ppermute x36, starting transfers between devices, passed_along(): return lax.ppermute(array, axis, pairs)  69.5 us
    dot_general x24, matrix products, update(): jnp.dot(weights, innovation, precision=lax.Precision.HIGHEST, preferred_e...  37.5 us
    gather x24, local copies, waits for them, and re-layouts, on_device(): flat_state[obs_cells[section_num, owner_num]]  25 us
    dot_general x24, matrix products, update(): jnp.dot(state_anom, anomaly.T, precision=lax.Precision.HIGHEST, preferred...  15.7 us
    mul x48, other arithmetic, taper(): weight_l[:, None, None, :] * weight_x[None, :, None, :]  12.5 us
  transfers between devices with their start and end apart: 40, of which 18 were waited for; matrix products, arithmetic and copies ran while one was open for 8% of the time, Pallas kernels for 0%

commit v1 on v0

v1 whole, which is shorter than its diff:
```python
import functools

import jax
import jax.numpy as jnp
from jax import lax
from jax.experimental import pallas as pl
from jax.experimental.pallas import tpu as pltpu
from jax.sharding import PartitionSpec as P

NU_COEF = 0.2
DAMP_COEF = 0.3
VERT_COEF = 0.6


def passed(array, axis, by):
    count = lax.axis_size(axis)
    return lax.ppermute(array, axis, [(i, i + by) for i in range(count) if 0 <= i + by < count])


def advance(prior_state, east_vel, north_vel):
    east_cells = jnp.concatenate([prior_state[:, 1:], passed(prior_state[:, :1], "tx", -1)], axis=1)
    west_cells = jnp.concatenate([passed(prior_state[:, -1:], "tx", 1), prior_state[:, :-1]], axis=1)
    north_cells = jnp.concatenate([prior_state[:, :, 1:], passed(prior_state[:, :, :1], "ty", -1)], axis=2)
    south_cells = jnp.concatenate([passed(prior_state[:, :, -1:], "ty", 1), prior_state[:, :, :-1]], axis=2)
    east_speed = east_vel[..., None]
    north_speed = north_vel[..., None]
    return (
        prior_state
        + NU_COEF * (east_cells + west_cells + north_cells + south_cells - 4.0 * prior_state)
        - 0.5 * east_speed * (east_cells - west_cells)
        - 0.5 * north_speed * (north_cells - south_cells)
        - DAMP_COEF * jnp.tanh(prior_state)
    )


def positions(tile_id, obs_cell, size_x, size_y, tiles_y):
    tile_i = tile_id // tiles_y
    tile_j = tile_id % tiles_y
    obs_level = obs_cell // (size_x * size_y)
    remain = obs_cell % (size_x * size_y)
    obs_x = tile_i * size_x + remain // size_y
    obs_y = tile_j * size_y + remain % size_y
    return (obs_level, obs_x, obs_y)


def spread_kernel(ntx, nty, column_ref, row_ref, mine_ref, out_ref, rows_ref, outgo_ref, income_ref,
                  send_a, recv_a, send_b, recv_b, send_c, recv_c, send_d, recv_d):
    mesh_ids = pl.DeviceIdType.MESH
    i = lax.axis_index("tx")
    j = lax.axis_index("ty")
    sections, owners = 3, column_ref.shape[1]
    sections = column_ref.shape[0]
    halves = owners * 2
    share = halves // ntx
    row_peers = [lax.rem(j + k, nty) for k in range(1, nty)]
    col_peers = [lax.rem(i + k, ntx) for k in range(1, ntx)]
    barrier = pltpu.get_barrier_semaphore()
    for t in row_peers:
        pl.semaphore_signal(barrier, inc=1, device_id=(i, t), device_id_type=mesh_ids)
    for c in col_peers:
        pl.semaphore_signal(barrier, inc=1, device_id=(c, j), device_id_type=mesh_ids)
    pl.semaphore_wait(barrier, nty - 1 + ntx - 1)

    sent = []
    for k, t in enumerate(row_peers):
        copy = pltpu.make_async_remote_copy(
            mine_ref.at[t], rows_ref.at[j], send_a.at[k], recv_a.at[j],
            device_id=(i, t), device_id_type=mesh_ids)
        copy.start()
        sent.append(copy)
    rows_ref[j] = mine_ref[j]
    for k, t in enumerate(row_peers):
        pltpu.make_async_remote_copy(
            mine_ref.at[t], rows_ref.at[t], send_a.at[k], recv_a.at[t],
            device_id=(i, t), device_id_type=mesh_ids).wait_recv()

    for s in range(sections):
        for o in range(owners):
            here = column_ref[s, o] == i
            for half in range(2):
                h = 2 * o + half
                outgo_ref[h // share, h % share, s] = jnp.where(here, rows_ref[row_ref[s, o], s, half], 0.0)
    for k, c in enumerate(col_peers):
        copy = pltpu.make_async_remote_copy(
            outgo_ref.at[c], income_ref.at[i], send_b.at[k], recv_b.at[i],
            device_id=(c, j), device_id_type=mesh_ids)
        copy.start()
        sent.append(copy)
    total = outgo_ref[i]
    for k, c in enumerate(col_peers):
        pltpu.make_async_remote_copy(
            outgo_ref.at[c], income_ref.at[c], send_b.at[k], recv_b.at[c],
            device_id=(c, j), device_id_type=mesh_ids).wait_recv()
        total = total + income_ref[c]
    out_ref[i, j] = total

    for k, t in enumerate(row_peers):
        copy = pltpu.make_async_remote_copy(
            out_ref.at[i, j], out_ref.at[i, j], send_c.at[k], recv_c.at[j],
            device_id=(i, t), device_id_type=mesh_ids)
        copy.start()
        sent.append(copy)
    for k, t in enumerate(row_peers):
        pltpu.make_async_remote_copy(
            out_ref.at[i, t], out_ref.at[i, t], send_c.at[k], recv_c.at[t],
            device_id=(i, t), device_id_type=mesh_ids).wait_recv()

    held = [i]
    count = 0
    bit = ntx // 2
    while bit >= 1:
        def flip(b, bit=bit):
            return b + bit - 2 * bit * lax.rem(b // bit, 2)
        partner = flip(i)
        for b in held:
            copy = pltpu.make_async_remote_copy(
                out_ref.at[b], out_ref.at[b], send_d.at[count], recv_d.at[b],
                device_id=(partner, j), device_id_type=mesh_ids)
            copy.start()
            sent.append(copy)
            count += 1
        fresh = [flip(b) for b in held]
        for b in fresh:
            pltpu.make_async_remote_copy(
                out_ref.at[b], out_ref.at[b], send_d.at[0], recv_d.at[b],
                device_id=(partner, j), device_id_type=mesh_ids).wait_recv()
        held = held + fresh
        bit //= 2
    for copy in sent:
        copy.wait_send()


def spread(payload, owner_tiles, ntx, nty):
    sections, count, members = payload.shape
    owners = owner_tiles.shape[1]
    rows, lanes, share = count // nty, members // 2, owners * 2 // ntx
    mine = payload.reshape(sections, nty, rows, 2, lanes).transpose(1, 0, 3, 2, 4)
    dma = pltpu.SemaphoreType.DMA
    everything = pl.pallas_call(
        functools.partial(spread_kernel, ntx, nty),
        out_shape=jax.ShapeDtypeStruct((ntx, nty, share, sections, rows, lanes), jnp.float32),
        in_specs=[pl.BlockSpec(memory_space=pltpu.SMEM)] * 2 + [pl.BlockSpec(memory_space=pltpu.VMEM)],
        out_specs=pl.BlockSpec(memory_space=pltpu.VMEM),
        scratch_shapes=[
            pltpu.VMEM((nty, sections, 2, rows, lanes), jnp.float32),
            pltpu.VMEM((ntx, share, sections, rows, lanes), jnp.float32),
            pltpu.VMEM((ntx, share, sections, rows, lanes), jnp.float32),
            dma((nty,)), dma((nty,)), dma((ntx,)), dma((ntx,)),
            dma((nty,)), dma((nty,)), dma((ntx,)), dma((ntx,)),
        ],
        compiler_params=pltpu.CompilerParams(
            collective_id=0, has_side_effects=True, vmem_limit_bytes=24 * 2**20),
    )(owner_tiles // nty, owner_tiles % nty, mine)
    return everything


def terms(a):
    high = a.astype(jnp.bfloat16)
    return high, (a - high.astype(jnp.float32)).astype(jnp.bfloat16)


def update_kernel(chunk, reach_x, reach_y, state_ref, slots_ref, noise_ref, column_ref, line_ref, out_ref,
                  all_ref, anom_ref, innov_ref):
    ntx, nty, share, sections, rows, lanes = slots_ref.shape
    cells, members = state_ref.shape
    observed = noise_ref.shape[1]
    per = nty * rows
    for s in range(sections):
        for h in range(2 * observed // per):
            all_ref[pl.ds(s * observed + h // 2 * per, per), pl.ds(h % 2 * lanes, lanes)] = slots_ref[
                h // share, :, h % share, s].reshape(per, lanes)
    total = sections * observed + cells
    all_ref[pl.ds(sections * observed, cells), :] = state_ref[...]
    for s in range(sections):
        start = s * observed
        prior_obs = all_ref[pl.ds(start, observed), :]
        anomaly = prior_obs - jnp.mean(prior_obs, axis=1, keepdims=True)
        value = column_ref[pl.ds(start, observed), 3:4]
        error = column_ref[pl.ds(start, observed), 4:5]
        factor = 1.0 / (jnp.sum(anomaly * anomaly, axis=1, keepdims=True) + (members - 1) * error)
        innovation = (value + jnp.sqrt(error) * noise_ref[s] - prior_obs) * factor
        high, low = terms(anomaly)
        anom_ref[...] = jnp.concatenate([high, high, low], axis=1)
        high, low = terms(innovation)
        innov_ref[...] = jnp.concatenate([high, high, low], axis=0)
        level_o = line_ref[s, 0:1, :]
        x_o = line_ref[s, 1:2, :]
        y_o = line_ref[s, 2:3, :]

        def refresh(at):
            block = all_ref[pl.ds(at, chunk), :]
            level = column_ref[pl.ds(at, chunk), 0:1]
            x = column_ref[pl.ds(at, chunk), 1:2]
            y = column_ref[pl.ds(at, chunk), 2:3]
            high, low = terms(block - jnp.mean(block, axis=1, keepdims=True))
            covar = lax.dot_general(
                jnp.concatenate([high, low, high], axis=1), anom_ref[...], (((1,), (1,)), ((), ())),
                preferred_element_type=jnp.float32)
            near_x = jnp.maximum(0.0, 1.0 - jnp.abs(x - x_o) * (1.0 / reach_x))
            near_y = jnp.maximum(0.0, 1.0 - jnp.abs(y - y_o) * (1.0 / reach_y))
            near = near_x * near_y
            weights = covar * (near * near * jnp.where(level == level_o, 1.0, VERT_COEF))
            high, low = terms(weights)
            return block + jnp.dot(
                jnp.concatenate([high, low, high], axis=1), innov_ref[...], preferred_element_type=jnp.float32)

        first = start + observed
        if s + 1 < sections:
            @pl.loop(0, (total - first) // chunk)
            def _(n):
                at = pl.multiple_of(first + n * chunk, chunk)
                all_ref[pl.ds(at, chunk), :] = refresh(at)
        else:
            for n in range(cells // chunk):
                out_ref[pl.ds(n * chunk, chunk), :] = refresh(first + n * chunk)


def update(state, slots, noise, column, line, reach_x, reach_y):
    sections, observed, members = noise.shape
    cells = state.shape[0]
    total = sections * observed + cells
    chunk = 256
    whole = pl.BlockSpec(memory_space=pltpu.VMEM)
    return pl.pallas_call(
        functools.partial(update_kernel, chunk, reach_x, reach_y),
        out_shape=jax.ShapeDtypeStruct((cells, members), jnp.float32),
        in_specs=[whole] * 5,
        out_specs=whole,
        scratch_shapes=[
            pltpu.VMEM((total, members), jnp.float32),
            pltpu.VMEM((observed, 3 * members), jnp.bfloat16),
            pltpu.VMEM((3 * observed, members), jnp.bfloat16),
        ],
        compiler_params=pltpu.CompilerParams(vmem_limit_bytes=48 * 2**20),
    )(state, slots, noise, column, line)


def on_device(
    prior_state, east_vel, north_vel, owner_tiles, obs_cells, obs_value, obs_error, obs_pert
):
    levels, size_x, size_y, members = prior_state.shape
    section_count, owner_count, obs_count = obs_cells.shape
    ntx, nty = lax.axis_size("tx"), lax.axis_size("ty")
    column_idx = lax.axis_index("tx")
    row_idx = lax.axis_index("ty")
    my_tile = column_idx * nty + row_idx
    cells = levels * size_x * size_y
    state = advance(prior_state, east_vel, north_vel).reshape(cells, members)

    mine = owner_tiles == my_tile
    my_cells = jnp.sum(jnp.where(mine[:, :, None], obs_cells, 0), axis=1)
    chosen = (my_cells.reshape(-1)[:, None] == jnp.arange(cells)[None, :]).astype(jnp.float32)
    payload = jnp.dot(chosen, state, precision=lax.Precision.HIGHEST)
    slots = spread(payload.reshape(section_count, obs_count, members), owner_tiles, ntx, nty)

    level_o, x_o, y_o = positions(owner_tiles[:, :, None], obs_cells, size_x, size_y, nty)
    own = jnp.arange(cells, dtype=jnp.int32)
    level_c = own // (size_x * size_y)
    x_c = column_idx * size_x + own % (size_x * size_y) // size_y
    y_c = row_idx * size_y + own % size_y
    zero = jnp.zeros((cells,), jnp.float32)
    column = jnp.stack([
        jnp.concatenate([a.reshape(-1).astype(jnp.float32), b.astype(jnp.float32)])
        for a, b in ((level_o, level_c), (x_o, x_c), (y_o, y_c), (obs_value, zero), (obs_error, zero))
    ], axis=1)
    line = jnp.stack([a.reshape(section_count, -1).astype(jnp.float32) for a in (level_o, x_o, y_o)], axis=1)
    noise = obs_pert.reshape(section_count, owner_count * obs_count, members)
    out = update(state, slots, noise, column, line, 3.0 * size_x, 3.0 * size_y)
    return out.reshape(levels, size_x, size_y, members)


def solution(mesh):
    placed = (
        P(None, "tx", "ty", None),
        P(None, "tx", "ty"),
        P(None, "tx", "ty"),
        P(),
        P(),
        P(),
        P(),
        P(),
    )
    return jax.shard_map(
        on_device, mesh=mesh, in_specs=placed, out_specs=P(None, "tx", "ty", None), check_vma=False
    )
```

time: 557 us -> 118 us (0.21)
  the two profiles are of different devices: /device:TPU:4 before, /device:TPU:13 now
where the time goes in v1:
time: 118 us; the launch traced here: 116 us
  Pallas kernels  92.4 us (78%)
  starting transfers between devices  12.3 us (10%)
  local copies, waits for them, and re-layouts  8.16 us (7%)
  other arithmetic  2.56 us (2%)
    pallas_call x1, Pallas kernels, spread(): pl.pallas_call(functools.partial(spread_kernel, ntx, nty), out_shape=jax....  57.1 us
    pallas_call x1, Pallas kernels, update(): pl.pallas_call(functools.partial(update_kernel, chunk, reach_x, reach_y),...  35.3 us
    ppermute x4, starting transfers between devices, passed(): lax.ppermute(array, axis, [(i, i + by) for i in range(count) if 0 <= i +...  12.3 us
  transfers between devices with their start and end apart: 4, of which 0 were waited for; matrix products, arithmetic and copies ran while one was open for 6% of the time, Pallas kernels for 0%

profile of v1, /device:TPU:13, one launch (start us, length us, event | category | flops | bytes accessed | tf_op | source)
XLA Modules:
  0.0 116.4 jit_solution(1339999868902259258)
XLA Ops:
  0.0 0.0 copy-start.7
  0.0 0.0 copy-start.8
  0.0 0.0 copy-start.9
  0.0 0.0 copy-start.4
  0.0 0.0 copy-start.5
  0.0 0.0 copy-start.6
  0.0 1.0 fusion.33
  1.1 2.1 %collective-permute-start.2 = (f32[2,8,1,256]{3,2,1,0:T(1,128)S(1)}, f32[2,8,1,256]{3,2,1,0:T(1,128)S(1)}, u32[]{:S(2)}, u32[]{:S(2)}) collective-permute-start(f32[2,8,1,256]{3,2,1,0:T(1,128)S(1)} %get-tuple-element.15), channel_id=1, source_target_pairs={{1,0},{2,1},{3,2},{4,3},{5,4},{6,5},{7,6},{9,8},{10,9},{11,10},{12... | collective-permute-start | bytes 49160 | tf_op jit(solution)/shard_map/ppermute | solution.py:17
  3.2 4.0 %collective-permute-start.3 = (f32[2,8,1,256]{3,2,1,0:T(1,128)S(1)}, f32[2,8,1,256]{3,2,1,0:T(1,128)S(1)}, u32[]{:S(2)}, u32[]{:S(2)}) collective-permute-start(f32[2,8,1,256]{3,2,1,0:T(1,128)S(1)} %get-tuple-element.16), channel_id=1, source_target_pairs={{0,1},{1,2},{2,3},{3,4},{4,5},{5,6},{6,7},{8,9},{9,10},{10,11},{11... | collective-permute-start | bytes 49160 | tf_op jit(solution)/shard_map/ppermute | solution.py:17
  7.3 0.9 fusion.31
  8.2 3.1 %collective-permute-start = (f32[2,1,32,256]{3,2,1,0:T(8,128)S(1)}, f32[2,1,32,256]{3,2,1,0:T(8,128)S(1)}, u32[]{:S(2)}, u32[]{:S(2)}) collective-permute-start(f32[2,1,32,256]{3,2,1,0:T(8,128)S(1)} %get-tuple-element.11), channel_id=1, source_target_pairs={{8,0},{16,8},{24,16},{9,1},{17,9},{25,17},{10,2},{18,10},{26,18},{... | collective-permute-start | bytes 196616 | tf_op jit(solution)/shard_map/ppermute | solution.py:17
  11.3 3.0 %collective-permute-start.1 = (f32[2,1,32,256]{3,2,1,0:T(8,128)S(1)}, f32[2,1,32,256]{3,2,1,0:T(8,128)S(1)}, u32[]{:S(2)}, u32[]{:S(2)}) collective-permute-start(f32[2,1,32,256]{3,2,1,0:T(8,128)S(1)} %get-tuple-element.12), channel_id=1, source_target_pairs={{0,8},{8,16},{16,24},{1,9},{9,17},{17,25},{2,10},{10,18},{18,26},{... | collective-permute-start | bytes 196616 | tf_op jit(solution)/shard_map/ppermute | solution.py:17
  14.4 0.0 copy-start
  14.4 2.3 %fusion.30 = (f32[2,7,32,256]{3,2,1,0:T(8,128)}, f32[2,7,32,256]{3,2,1,0:T(8,128)}) fusion(f32[2,8,32,256]{3,2,1,0:T(8,128)} %param.8), kind=kLoop, calls=%fused_computation.76 | loop fusion | bytes 1835008 | tf_op jit(solution)/shard_map/slice | solution.py:21
  16.7 2.2 %fusion.32 = (f32[2,8,31,256]{3,2,1,0:T(8,128)S(1)}, f32[2,8,31,256]{3,2,1,0:T(8,128)}) fusion(f32[2,8,32,256]{3,2,1,0:T(8,128)} %param.8), kind=kLoop, calls=%fused_computation.78 | loop fusion | bytes 2031616 | tf_op jit(solution)/shard_map/slice | solution.py:23
  18.9 0.0 copy-done.7
  19.0 0.0 copy-done.8
  19.0 0.0 copy-done.9
  19.0 0.6 broadcast_multiply_fusion
  19.6 0.0 copy-done.4
  19.6 0.1 fusion.7
  19.8 0.0 copy-done.5
  19.8 0.0 copy-done.6
  19.9 0.1 eq.49
  20.0 0.1 stack.29
  20.1 0.6 copy.22.column_ref
  20.7 0.0 collective-permute-done.2
  20.7 0.0 copy-start.2
  20.7 0.0 collective-permute-done.3
  20.7 0.0 copy-start.3
  20.7 0.0 collective-permute-done
  20.8 0.0 collective-permute-done.1
  20.8 0.0 copy-start.1
  20.8 0.5 copy-done.2
  21.3 0.0 copy-done.3
  21.3 0.1 copy-done.1
  21.4 0.0 copy-done
  21.4 1.8 %multiply_subtract_fusion = f32[2,8,32,256]{3,2,1,0:T(8,128)S(1)} fusion(f32[2,8,32,256]{3,2,1,0:T(8,128)S(1)} %copy-done, f32[2,8,31,256]{3,2,1,0:T(8,128)} %get-tuple-element.14, f32[2,8,1,256]{3,2,1,0:T(1,128)} %copy-done.3, f32[2,8,1,256]{3,2,1,0:T(1,128)} %copy-done.2, f32[2,8,31,256]{3,2,1,0:T(8,128)S(1)} %get-tuple-element.13, ...), kind=kLoop, calls=%fused_computation.7 | loop fusion | flops 2490368 | bytes 3149824 | tf_op jit(solution)/shard_map/sub | solution.py:28
  23.2 0.2 copy.24
  23.4 0.6 convolution_bitcast_fusion.mine_ref
  24.0 57.1 %shard_map.82.slots_ref = f32[4,8,4,3,16,128]{5,4,3,2,1,0:T(8,128)S(1)} custom-call(s32[3,8]{1,0:T(4,128)S(1)} %get-tuple-element.22.column_ref, s32[3,8]{1,0:T(4,128)S(1)} %get-tuple-element.6.row_ref, f32[8,3,2,16,128]{4,3,2,1,0:T(8,128)S(1)} %convolution_bitcast_fusion.mine_ref), custom_call_target="tpu_custom_call" | custom-call | tf_op jit(solution)/shard_map/pallas_call | solution.py:139
  81.1 35.3 %shard_map.83 = f32[512,256]{1,0:T(8,128)} custom-call(f32[512,256]{1,0:T(8,128)S(1)} %bitcast.26, f32[4,8,4,3,16,128]{5,4,3,2,1,0:T(8,128)S(1)} %shard_map.82.slots_ref, f32[3,1024,256]{2,1,0:T(8,128)} %bitcast.27, f32[3584,5]{1,0:T(8,128)S(1)} %copy.22.column_ref, f32[3,3,1024]{2,1,0:T(4,128)S(1)} %pad_maximum_fusion.4.line_ref), custom_call_target="tpu_custom_call" | custom-call | tf_op jit(solution)/shard_map/pallas_call | solution.py:224
  (17 shorter events, 0.2 us)
Async XLA Ops:
  0.0 19.0 %copy-start.7 = (s32[3,8]{1,0:T(4,128)S(1)}, s32[3,8]{1,0:T(4,128)}, u32[]{:S(2)}) copy-start(s32[3,8]{1,0:T(4,128)} %param.11) | copy-start | bytes 292
  0.0 19.0 %copy-start.8 = (f32[2,8,32]{2,1,0:T(8,128)S(1)}, f32[2,8,32]{2,1,0:T(8,128)}, u32[]{:S(2)}) copy-start(f32[2,8,32]{2,1,0:T(8,128)} %param.10) | copy-start | bytes 6148
  0.0 19.0 %copy-start.9 = (f32[2,8,32]{2,1,0:T(8,128)S(1)}, f32[2,8,32]{2,1,0:T(8,128)}, u32[]{:S(2)}) copy-start(f32[2,8,32]{2,1,0:T(8,128)} %param.9) | copy-start | bytes 6148
  0.0 19.6 %copy-start.4 = (s32[3,8,128]{2,1,0:T(8,128)S(1)}, s32[3,8,128]{2,1,0:T(8,128)}, u32[]{:S(2)}) copy-start(s32[3,8,128]{2,1,0:T(8,128)} %param.12) | copy-start | bytes 36868
  0.0 19.8 %copy-start.5 = (f32[3,8,128]{2,1,0:T(8,128)S(1)}, f32[3,8,128]{2,1,0:T(8,128)}, u32[]{:S(2)}) copy-start(f32[3,8,128]{2,1,0:T(8,128)} %param.13) | copy-start | bytes 36868
  0.0 19.8 %copy-start.6 = (f32[3,8,128]{2,1,0:T(8,128)S(1)}, f32[3,8,128]{2,1,0:T(8,128)}, u32[]{:S(2)}) copy-start(f32[3,8,128]{2,1,0:T(8,128)} %param.14) | copy-start | bytes 36868
  1.1 19.6 %collective-permute-start.2 = (f32[2,8,1,256]{3,2,1,0:T(1,128)S(1)}, f32[2,8,1,256]{3,2,1,0:T(1,128)S(1)}, u32[]{:S(2)}, u32[]{:S(2)}) collective-permute-start(f32[2,8,1,256]{3,2,1,0:T(1,128)S(1)} %get-tuple-element.15), channel_id=1, source_target_pairs={{1,0},{2,1},{3,2},{4,3},{5,4},{6,5},{7,6},{9,8},{10,9},{11,10},{12... | collective-permute-start | bytes 49160 | tf_op jit(solution)/shard_map/ppermute | solution.py:17
  3.2 17.5 %collective-permute-start.3 = (f32[2,8,1,256]{3,2,1,0:T(1,128)S(1)}, f32[2,8,1,256]{3,2,1,0:T(1,128)S(1)}, u32[]{:S(2)}, u32[]{:S(2)}) collective-permute-start(f32[2,8,1,256]{3,2,1,0:T(1,128)S(1)} %get-tuple-element.16), channel_id=1, source_target_pairs={{0,1},{1,2},{2,3},{3,4},{4,5},{5,6},{6,7},{8,9},{9,10},{10,11},{11... | collective-permute-start | bytes 49160 | tf_op jit(solution)/shard_map/ppermute | solution.py:17
  8.2 12.6 %collective-permute-start = (f32[2,1,32,256]{3,2,1,0:T(8,128)S(1)}, f32[2,1,32,256]{3,2,1,0:T(8,128)S(1)}, u32[]{:S(2)}, u32[]{:S(2)}) collective-permute-start(f32[2,1,32,256]{3,2,1,0:T(8,128)S(1)} %get-tuple-element.11), channel_id=1, source_target_pairs={{8,0},{16,8},{24,16},{9,1},{17,9},{25,17},{10,2},{18,10},{26,18},{... | collective-permute-start | bytes 196616 | tf_op jit(solution)/shard_map/ppermute | solution.py:17
  11.3 9.4 %collective-permute-start.1 = (f32[2,1,32,256]{3,2,1,0:T(8,128)S(1)}, f32[2,1,32,256]{3,2,1,0:T(8,128)S(1)}, u32[]{:S(2)}, u32[]{:S(2)}) collective-permute-start(f32[2,1,32,256]{3,2,1,0:T(8,128)S(1)} %get-tuple-element.12), channel_id=1, source_target_pairs={{0,8},{8,16},{16,24},{1,9},{9,17},{17,25},{2,10},{10,18},{18,26},{... | collective-permute-start | bytes 196616 | tf_op jit(solution)/shard_map/ppermute | solution.py:17
  14.4 7.0 %copy-start = (f32[2,8,32,256]{3,2,1,0:T(8,128)S(1)}, f32[2,8,32,256]{3,2,1,0:T(8,128)}, u32[]{:S(2)}) copy-start(f32[2,8,32,256]{3,2,1,0:T(8,128)} %param.8) | copy-start | bytes 1572868
  20.7 0.6 copy-start.2
  20.7 0.6 copy-start.3
  20.8 0.6 copy-start.1

commit v2 on v1

v2 whole, which is shorter than its diff:
```python
import functools

import jax
import jax.numpy as jnp
from jax import lax
from jax.experimental import pallas as pl
from jax.experimental.pallas import tpu as pltpu
from jax.sharding import PartitionSpec as P

NU_COEF = 0.2
DAMP_COEF = 0.3
VERT_COEF = 0.6


def positions(tile_id, obs_cell, size_x, size_y, tiles_y):
    tile_i = tile_id // tiles_y
    tile_j = tile_id % tiles_y
    obs_level = obs_cell // (size_x * size_y)
    remain = obs_cell % (size_x * size_y)
    obs_x = tile_i * size_x + remain // size_y
    obs_y = tile_j * size_y + remain % size_y
    return (obs_level, obs_x, obs_y)


def spread_kernel(ntx, nty, column_ref, row_ref, prior_ref, speed_ref, mycell_ref, state_ref, out_ref,
                  pad_ref, edge_ref, halo_x_ref, halo_y_ref, mine_ref, rows_refs, outgo_ref, income_ref,
                  send_h, recv_h, send_a, recv_a, send_b, recv_b, send_c, recv_c, send_d, recv_d):
    mesh_ids = pl.DeviceIdType.MESH
    i = lax.axis_index("tx")
    j = lax.axis_index("ty")
    levels, size_x, size_y, members = prior_ref.shape
    cells = levels * size_x * size_y
    sections, owners = column_ref.shape
    share, rows, lanes = out_ref.shape[3:]
    row_peers = [lax.rem(j + k, nty) for k in range(1, nty)]
    col_peers = [lax.rem(i + k, ntx) for k in range(1, ntx)]
    barrier = pltpu.get_barrier_semaphore()
    for t in row_peers:
        pl.semaphore_signal(barrier, inc=1, device_id=(i, t), device_id_type=mesh_ids)
    for c in col_peers:
        pl.semaphore_signal(barrier, inc=1, device_id=(c, j), device_id_type=mesh_ids)
    for lev in range(levels):
        for x in range(size_x):
            edge_ref[0, lev, x:x + 1, :] = prior_ref[lev, x, size_y - 1:size_y, :]
            edge_ref[1, lev, x:x + 1, :] = prior_ref[lev, x, 0:1, :]
    pl.semaphore_wait(barrier, nty - 1 + ntx - 1)

    def sending(src, dst, send_sem, recv_sem, to):
        copy = pltpu.make_async_remote_copy(src, dst, send_sem, recv_sem, device_id=to, device_id_type=mesh_ids)
        copy.start()
        sent.append(copy)

    def arrived(ref, send_sem, recv_sem, to):
        pltpu.make_async_remote_copy(
            ref, ref, send_sem, recv_sem, device_id=to, device_id_type=mesh_ids).wait_recv()

    sent = []
    east, west = (lax.rem(i + 1, ntx), j), (lax.rem(i + ntx - 1, ntx), j)
    north, south = (i, lax.rem(j + 1, nty)), (i, lax.rem(j + nty - 1, nty))
    sending(prior_ref.at[:, size_x - 1], halo_x_ref.at[0], send_h.at[0], recv_h.at[0], east)
    sending(prior_ref.at[:, 0], halo_x_ref.at[1], send_h.at[1], recv_h.at[1], west)
    sending(edge_ref.at[0], halo_y_ref.at[0], send_h.at[2], recv_h.at[2], north)
    sending(edge_ref.at[1], halo_y_ref.at[1], send_h.at[3], recv_h.at[3], south)
    prior = prior_ref[...]
    pad_ref[:, :, 8:8 + size_y, :] = prior
    arrived(halo_x_ref.at[0], send_h.at[0], recv_h.at[0], west)
    arrived(halo_x_ref.at[1], send_h.at[1], recv_h.at[1], east)
    arrived(halo_y_ref.at[0], send_h.at[2], recv_h.at[2], south)
    arrived(halo_y_ref.at[1], send_h.at[3], recv_h.at[3], north)
    for lev in range(levels):
        for x in range(size_x):
            pad_ref[lev, x, 7:8, :] = jnp.where(j == 0, 0.0, halo_y_ref[0, lev, x:x + 1, :])
            pad_ref[lev, x, 8 + size_y:9 + size_y, :] = jnp.where(
                j == nty - 1, 0.0, halo_y_ref[1, lev, x:x + 1, :])
    west_halo = jnp.where(i == 0, 0.0, halo_x_ref[0])[:, None]
    east_halo = jnp.where(i == ntx - 1, 0.0, halo_x_ref[1])[:, None]
    flat = lambda a: a.reshape(cells, members)
    east_cells = flat(jnp.concatenate([prior[:, 1:], east_halo], axis=1))
    west_cells = flat(jnp.concatenate([west_halo, prior[:, :-1]], axis=1))
    north_cells = flat(pad_ref[:, :, 9:9 + size_y, :])
    south_cells = flat(pad_ref[:, :, 7:7 + size_y, :])
    prior = flat(prior)
    state_ref[...] = (
        prior
        + NU_COEF * (east_cells + west_cells + north_cells + south_cells - 4.0 * prior)
        - 0.5 * speed_ref[:, 0:1] * (east_cells - west_cells)
        - 0.5 * speed_ref[:, 1:2] * (north_cells - south_cells)
        - DAMP_COEF * jnp.tanh(prior)
    )
    count = nty * rows
    for s in range(sections):
        places = lax.broadcasted_iota(jnp.int32, (count, cells), 1)
        chosen = jnp.where(mycell_ref[s * count:(s + 1) * count, :] == places, 1.0, 0.0)
        payload = jnp.dot(
            chosen, state_ref[...], precision=lax.Precision.HIGHEST, preferred_element_type=jnp.float32)
        for half in range(2):
            mine_ref[s, :, half] = payload[:, half * lanes:(half + 1) * lanes].reshape(nty, rows, lanes)
        for k, t in enumerate(row_peers):
            sending(mine_ref.at[s, t], rows_refs[s].at[j], send_a.at[s, k], recv_a.at[s, j], (i, t))
        rows_refs[s][j] = mine_ref[s, j]

    for s in range(sections):
        for k, t in enumerate(row_peers):
            arrived(rows_refs[s].at[t], send_a.at[s, k], recv_a.at[s, t], (i, t))
        for o in range(owners):
            here = column_ref[s, o] == i
            for half in range(2):
                h = 2 * o + half
                outgo_ref[s, h // share, h % share] = jnp.where(here, rows_refs[s][row_ref[s, o], half], 0.0)
        for k, c in enumerate(col_peers):
            sending(outgo_ref.at[s, c], income_ref.at[s, i], send_b.at[s, k], recv_b.at[s, i], (c, j))

    for s in range(sections):
        total = outgo_ref[s, i]
        for k, c in enumerate(col_peers):
            arrived(income_ref.at[s, c], send_b.at[s, k], recv_b.at[s, c], (c, j))
            total = total + income_ref[s, c]
        out_ref[s, i, j] = total
        for k, t in enumerate(row_peers):
            sending(out_ref.at[s, i, j], out_ref.at[s, i, j], send_c.at[s, k], recv_c.at[s, j], (i, t))

    def flip(b, bit):
        return b + bit - 2 * bit * lax.rem(b // bit, 2)

    stages = []
    held = [i]
    bit = ntx // 2
    while bit >= 1:
        stages.append((bit, held))
        held = held + [flip(b, bit) for b in held]
        bit //= 2
    for number, (bit, held) in enumerate(stages):
        partner = (flip(i, bit), j)
        for s in range(sections):
            if number == 0:
                for k, t in enumerate(row_peers):
                    arrived(out_ref.at[s, i, t], send_c.at[s, k], recv_c.at[s, t], (i, t))
            else:
                before, had = stages[number - 1]
                for b in had:
                    b = flip(b, before)
                    arrived(out_ref.at[s, b], send_d.at[s, 0], recv_d.at[s, b], partner)
            for n, b in enumerate(held):
                sending(out_ref.at[s, b], out_ref.at[s, b], send_d.at[s, len(held) - 1 + n], recv_d.at[s, b], partner)
    bit, held = stages[-1]
    for s in range(sections):
        for b in held:
            b = flip(b, bit)
            arrived(out_ref.at[s, b], send_d.at[s, 0], recv_d.at[s, b], (flip(i, bit), j))
    for copy in sent:
        copy.wait_send()


def spread(prior_state, speeds, my_cells, owner_tiles, ntx, nty):
    levels, size_x, size_y, members = prior_state.shape
    sections, owners = owner_tiles.shape
    count = my_cells.shape[0] // sections
    rows, lanes, share = count // nty, members // 2, owners * 2 // ntx
    dma = pltpu.SemaphoreType.DMA
    f32 = jnp.float32
    whole = pl.BlockSpec(memory_space=pltpu.VMEM)
    return pl.pallas_call(
        functools.partial(spread_kernel, ntx, nty),
        out_shape=(
            jax.ShapeDtypeStruct((levels * size_x * size_y, members), f32),
            jax.ShapeDtypeStruct((sections, ntx, nty, share, rows, lanes), f32),
        ),
        in_specs=[pl.BlockSpec(memory_space=pltpu.SMEM)] * 2 + [whole] * 3,
        out_specs=(whole, whole),
        scratch_shapes=[
            pltpu.VMEM((levels, size_x, size_y + 16, members), f32),
            pltpu.VMEM((2, levels, size_x, members), f32),
            pltpu.VMEM((2, levels, size_y, members), f32),
            pltpu.VMEM((2, levels, size_x, members), f32),
            pltpu.VMEM((sections, nty, 2, rows, lanes), f32),
            [pltpu.VMEM((nty, 2, rows, lanes), f32)] * sections,
            pltpu.VMEM((sections, ntx, share, rows, lanes), f32),
            pltpu.VMEM((sections, ntx, share, rows, lanes), f32),
            dma((4,)), dma((4,)),
            dma((sections, nty)), dma((sections, nty)), dma((sections, ntx)), dma((sections, ntx)),
            dma((sections, nty)), dma((sections, nty)), dma((sections, ntx)), dma((sections, ntx)),
        ],
        compiler_params=pltpu.CompilerParams(
            collective_id=0, has_side_effects=True, vmem_limit_bytes=32 * 2**20),
    )(owner_tiles // nty, owner_tiles % nty, prior_state, speeds, my_cells)


def terms(a):
    high = a.astype(jnp.bfloat16)
    return high, (a - high.astype(jnp.float32)).astype(jnp.bfloat16)


def update_kernel(chunk, reach_x, reach_y, state_ref, slots_ref, noise_ref, column_ref, line_ref, out_ref,
                  all_ref, anom_ref, innov_ref):
    sections, ntx, nty, share, rows, lanes = slots_ref.shape
    cells, members = state_ref.shape
    observed = noise_ref.shape[1]
    per = nty * rows
    for s in range(sections):
        for h in range(2 * observed // per):
            all_ref[pl.ds(s * observed + h // 2 * per, per), pl.ds(h % 2 * lanes, lanes)] = slots_ref[
                s, h // share, :, h % share].reshape(per, lanes)
    total = sections * observed + cells
    all_ref[pl.ds(sections * observed, cells), :] = state_ref[...]
    for s in range(sections):
        start = s * observed
        prior_obs = all_ref[pl.ds(start, observed), :]
        anomaly = prior_obs - jnp.mean(prior_obs, axis=1, keepdims=True)
        value = column_ref[pl.ds(start, observed), 3:4]
        error = column_ref[pl.ds(start, observed), 4:5]
        factor = 1.0 / (jnp.sum(anomaly * anomaly, axis=1, keepdims=True) + (members - 1) * error)
        innovation = (value + jnp.sqrt(error) * noise_ref[s] - prior_obs) * factor
        high, low = terms(anomaly)
        anom_ref[...] = jnp.concatenate([high, high, low], axis=1)
        high, low = terms(innovation)
        innov_ref[...] = jnp.concatenate([high, high, low], axis=0)
        level_o = line_ref[s, 0:1, :]
        x_o = line_ref[s, 1:2, :]
        y_o = line_ref[s, 2:3, :]

        def refresh(at):
            block = all_ref[pl.ds(at, chunk), :]
            level = column_ref[pl.ds(at, chunk), 0:1]
            x = column_ref[pl.ds(at, chunk), 1:2]
            y = column_ref[pl.ds(at, chunk), 2:3]
            high, low = terms(block - jnp.mean(block, axis=1, keepdims=True))
            covar = lax.dot_general(
                jnp.concatenate([high, low, high], axis=1), anom_ref[...], (((1,), (1,)), ((), ())),
                preferred_element_type=jnp.float32)
            near_x = jnp.maximum(0.0, 1.0 - jnp.abs(x - x_o) * (1.0 / reach_x))
            near_y = jnp.maximum(0.0, 1.0 - jnp.abs(y - y_o) * (1.0 / reach_y))
            near = near_x * near_y
            weights = covar * (near * near * jnp.where(level == level_o, 1.0, VERT_COEF))
            high, low = terms(weights)
            return block + jnp.dot(
                jnp.concatenate([high, low, high], axis=1), innov_ref[...], preferred_element_type=jnp.float32)

        first = start + observed
        if s + 1 < sections:
            @pl.loop(0, (total - first) // chunk)
            def _(n):
                at = pl.multiple_of(first + n * chunk, chunk)
                all_ref[pl.ds(at, chunk), :] = refresh(at)
        else:
            for n in range(cells // chunk):
                out_ref[pl.ds(n * chunk, chunk), :] = refresh(first + n * chunk)


def update(state, slots, noise, column, line, reach_x, reach_y):
    sections, observed, members = noise.shape
    cells = state.shape[0]
    total = sections * observed + cells
    chunk = 256
    whole = pl.BlockSpec(memory_space=pltpu.VMEM)
    return pl.pallas_call(
        functools.partial(update_kernel, chunk, reach_x, reach_y),
        out_shape=jax.ShapeDtypeStruct((cells, members), jnp.float32),
        in_specs=[whole] * 5,
        out_specs=whole,
        scratch_shapes=[
            pltpu.VMEM((total, members), jnp.float32),
            pltpu.VMEM((observed, 3 * members), jnp.bfloat16),
            pltpu.VMEM((3 * observed, members), jnp.bfloat16),
        ],
        compiler_params=pltpu.CompilerParams(vmem_limit_bytes=48 * 2**20),
    )(state, slots, noise, column, line)


def on_device(
    prior_state, east_vel, north_vel, owner_tiles, obs_cells, obs_value, obs_error, obs_pert
):
    levels, size_x, size_y, members = prior_state.shape
    section_count, owner_count, obs_count = obs_cells.shape
    ntx, nty = lax.axis_size("tx"), lax.axis_size("ty")
    column_idx = lax.axis_index("tx")
    row_idx = lax.axis_index("ty")
    my_tile = column_idx * nty + row_idx
    cells = levels * size_x * size_y

    mine = owner_tiles == my_tile
    my_cells = jnp.sum(jnp.where(mine[:, :, None], obs_cells, 0), axis=1)
    speeds = jnp.stack([east_vel.reshape(cells), north_vel.reshape(cells)], axis=1)
    state, slots = spread(prior_state, speeds, my_cells.reshape(-1, 1), owner_tiles, ntx, nty)

    level_o, x_o, y_o = positions(owner_tiles[:, :, None], obs_cells, size_x, size_y, nty)
    own = jnp.arange(cells, dtype=jnp.int32)
    level_c = own // (size_x * size_y)
    x_c = column_idx * size_x + own % (size_x * size_y) // size_y
    y_c = row_idx * size_y + own % size_y
    zero = jnp.zeros((cells,), jnp.float32)
    column = jnp.stack([
        jnp.concatenate([a.reshape(-1).astype(jnp.float32), b.astype(jnp.float32)])
        for a, b in ((level_o, level_c), (x_o, x_c), (y_o, y_c), (obs_value, zero), (obs_error, zero))
    ], axis=1)
    line = jnp.stack([a.reshape(section_count, -1).astype(jnp.float32) for a in (level_o, x_o, y_o)], axis=1)
    noise = obs_pert.reshape(section_count, owner_count * obs_count, members)
    out = update(state, slots, noise, column, line, 3.0 * size_x, 3.0 * size_y)
    return out.reshape(levels, size_x, size_y, members)


def solution(mesh):
    placed = (
        P(None, "tx", "ty", None),
        P(None, "tx", "ty"),
        P(None, "tx", "ty"),
        P(),
        P(),
        P(),
        P(),
        P(),
    )
    return jax.shard_map(
        on_device, mesh=mesh, in_specs=placed, out_specs=P(None, "tx", "ty", None), check_vma=False
    )
```

time: 118 us -> 92.5 us (0.78)
  starting transfers between devices: 12.3 us -> 0 us
  Pallas kernels: 92.4 us -> 85.5 us
  local copies, waits for them, and re-layouts: 8.16 us -> 4.01 us
    ppermute x4 -> x0, starting transfers between devices: 12.3 us -> none  [passed(): lax.ppermute(array, axis, [(i, i + by) for i in range(count) if 0 <= i +...]
    pallas_call x1, Pallas kernels: 57.1 us -> 50.5 us  [spread(): pl.pallas_call(functools.partial(spread_kernel, ntx, nty), out_shape=(jax...]
    slice x4 -> x0, local copies, waits for them, and re-layouts: 6.49 us -> none  [the longest x1 2.32 us: advance(): prior_state[:, 1:]]
    sub x1 -> x0, other arithmetic: 1.78 us -> none  [advance(): prior_state + NU_COEF * (east_cells + west_cells + north_cells + south_ce...]
    another operation x0 -> x3, local copies, waits for them, and re-layouts: none -> 1.7 us  [on_device(): jnp.stack([east_vel.reshape(cells), north_vel.reshape(cells)], axis=1)]
    concatenate x2, local copies, waits for them, and re-layouts: 0.01 us -> 1.42 us  [on_device(): jnp.concatenate([a.reshape(-1).astype(jnp.float32), b.astype(jnp.float32)])]
  transfers between devices with their start and end apart: 4 -> 0, of which waited for: 0 -> 0; matrix products, arithmetic and copies ran while one was open for 6% -> 0% of each run, Pallas kernels for 0% -> 0%
where the time goes in v2:
time: 92.5 us; the launch traced here: 92 us
  Pallas kernels  85.5 us (92%)
  local copies, waits for them, and re-layouts  4.01 us (4%)
  other arithmetic  2.32 us (3%)
    pallas_call x1, Pallas kernels, spread(): pl.pallas_call(functools.partial(spread_kernel, ntx, nty), out_shape=(jax...  50.5 us
    pallas_call x1, Pallas kernels, update(): pl.pallas_call(functools.partial(update_kernel, chunk, reach_x, reach_y),...  35.1 us

profile of v2, /device:TPU:13, one launch (start us, length us, event | category | flops | bytes accessed | tf_op | source)
XLA Modules:
  0.0 92.0 jit_solution(7937916110260558488)
XLA Ops:
  0.0 0.0 copy-start
  0.0 0.7 broadcast_compare_fusion
  0.8 0.8 stack_reshape.6
  1.5 0.8 stack_reshape.7
  2.3 0.7 broadcast_multiply_fusion
  3.0 0.7 concatenate.18
  3.8 0.7 concatenate.19
  4.5 0.8 fusion.4
  5.4 0.1 stack.33
  5.6 0.1 copy.21
  5.7 0.1 copy.17.speed_ref
  5.9 0.6 copy.19.column_ref
  6.4 0.0 copy-done
  6.5 50.5 %shard_map.82 = (f32[512,256]{1,0:T(8,128)S(1)}, f32[3,4,8,4,16,128]{5,4,3,2,1,0:T(8,128)S(1)}) custom-call(s32[3,8]{1,0:T(4,128)S(1)} %get-tuple-element.18.column_ref, s32[3,8]{1,0:T(4,128)S(1)} %get-tuple-element.10.row_ref, f32[2,8,32,256]{3,2,1,0:T(8,128)S(1)} %copy-done, f32[512,2]{1,0:T(8,128)S(1)} %copy.17.speed_ref, s32[384,1]{1,0:T(8,128)S(1)} %bitcast.16), custom_call_target="tpu_custom_call" | custom-call | tf_op jit(solution)/shard_map/pallas_call | solution.py:162
  56.9 35.1 %shard_map.83 = f32[512,256]{1,0:T(8,128)} custom-call(f32[512,256]{1,0:T(8,128)S(1)} %get-tuple-element.7.state_ref, f32[3,4,8,4,16,128]{5,4,3,2,1,0:T(8,128)S(1)} %get-tuple-element.8.slots_ref, f32[3,1024,256]{2,1,0:T(8,128)} %bitcast.17, f32[3584,5]{1,0:T(8,128)S(1)} %copy.19.column_ref, f32[3,3,1024]{2,1,0:T(4,128)S(1)} %pad_maximum_fusion.line_ref), custom_call_target="tpu_custom_call" | custom-call | tf_op jit(solution)/shard_map/pallas_call | solution.py:255
  (14 shorter events, 0.2 us)
Async XLA Ops:
  0.0 6.4 %copy-start = (f32[2,8,32,256]{3,2,1,0:T(8,128)S(1)}, f32[2,8,32,256]{3,2,1,0:T(8,128)}, u32[]{:S(2)}) copy-start(f32[2,8,32,256]{3,2,1,0:T(8,128)} %prior_ref.1) | copy-start | bytes 1572868

commit v3 on v2

--- a/solution.py
+++ b/solution.py
@@ -190,8 +190,8 @@
     return high, (a - high.astype(jnp.float32)).astype(jnp.bfloat16)
 
 
-def update_kernel(chunk, reach_x, reach_y, state_ref, slots_ref, noise_ref, column_ref, line_ref, out_ref,
-                  all_ref, anom_ref, innov_ref):
+def update_kernel(chunk, reach_x, reach_y, state_ref, slots_ref, noise_ref, line_ref, own_ref, out_ref,
+                  column_ref, all_ref, anom_ref, innov_ref):
     sections, ntx, nty, share, rows, lanes = slots_ref.shape
     cells, members = state_ref.shape
     observed = noise_ref.shape[1]
@@ -202,6 +202,9 @@
                 s, h // share, :, h % share].reshape(per, lanes)
     total = sections * observed + cells
     all_ref[pl.ds(sections * observed, cells), :] = state_ref[...]
+    for s in range(sections):
+        column_ref[pl.ds(s * observed, observed), :] = line_ref[s].T
+    column_ref[pl.ds(sections * observed, cells), :] = own_ref[...].T
     for s in range(sections):
         start = s * observed
         prior_obs = all_ref[pl.ds(start, observed), :]
@@ -237,16 +240,15 @@
 
         first = start + observed
         if s + 1 < sections:
-            @pl.loop(0, (total - first) // chunk)
-            def _(n):
-                at = pl.multiple_of(first + n * chunk, chunk)
+            for n in range((total - first) // chunk):
+                at = first + n * chunk
                 all_ref[pl.ds(at, chunk), :] = refresh(at)
         else:
             for n in range(cells // chunk):
                 out_ref[pl.ds(n * chunk, chunk), :] = refresh(first + n * chunk)
 
 
-def update(state, slots, noise, column, line, reach_x, reach_y):
+def update(state, slots, noise, line, own, reach_x, reach_y):
     sections, observed, members = noise.shape
     cells = state.shape[0]
     total = sections * observed + cells
@@ -258,12 +260,13 @@
         in_specs=[whole] * 5,
         out_specs=whole,
         scratch_shapes=[
+            pltpu.VMEM((total, 8), jnp.float32),
             pltpu.VMEM((total, members), jnp.float32),
             pltpu.VMEM((observed, 3 * members), jnp.bfloat16),
             pltpu.VMEM((3 * observed, members), jnp.bfloat16),
         ],
         compiler_params=pltpu.CompilerParams(vmem_limit_bytes=48 * 2**20),
-    )(state, slots, noise, column, line)
+    )(state, slots, noise, line, own)
 
 
 def on_device(
@@ -287,14 +290,11 @@
     level_c = own // (size_x * size_y)
     x_c = column_idx * size_x + own % (size_x * size_y) // size_y
     y_c = row_idx * size_y + own % size_y
-    zero = jnp.zeros((cells,), jnp.float32)
-    column = jnp.stack([
-        jnp.concatenate([a.reshape(-1).astype(jnp.float32), b.astype(jnp.float32)])
-        for a, b in ((level_o, level_c), (x_o, x_c), (y_o, y_c), (obs_value, zero), (obs_error, zero))
-    ], axis=1)
-    line = jnp.stack([a.reshape(section_count, -1).astype(jnp.float32) for a in (level_o, x_o, y_o)], axis=1)
+    rows_of = lambda parts: jnp.stack([a.astype(jnp.float32) for a in parts + parts[:8 - len(parts)]], axis=-2)
+    line = rows_of([a.reshape(section_count, -1) for a in (level_o, x_o, y_o, obs_value, obs_error)])
+    own = rows_of([level_c, x_c, y_c, x_c, y_c])
     noise = obs_pert.reshape(section_count, owner_count * obs_count, members)
-    out = update(state, slots, noise, column, line, 3.0 * size_x, 3.0 * size_y)
+    out = update(state, slots, noise, line, own, 3.0 * size_x, 3.0 * size_y)
     return out.reshape(levels, size_x, size_y, members)
 
 

time: 92.5 us -> 79.5 us (0.86)
  Pallas kernels: 85.5 us -> 72.9 us
    pallas_call x1, Pallas kernels: 35.1 us -> 22.5 us  [update(): pl.pallas_call(functools.partial(update_kernel, chunk, reach_x, reach_y),...]
    concatenate x2 -> x0, local copies, waits for them, and re-layouts: 1.42 us -> none  [on_device(): jnp.concatenate([a.reshape(-1).astype(jnp.float32), b.astype(jnp.float32)])]
    unnamed x4, local copies, waits for them, and re-layouts: 0.15 us -> 1.18 us
where the time goes in v3:
time: 79.5 us; the launch traced here: 79 us
  Pallas kernels  72.9 us (92%)
  local copies, waits for them, and re-layouts  3.79 us (5%)
  other arithmetic  2.21 us (3%)
    pallas_call x1, Pallas kernels, spread(): pl.pallas_call(functools.partial(spread_kernel, ntx, nty), out_shape=(jax...  50.4 us
    pallas_call x1, Pallas kernels, update(): pl.pallas_call(functools.partial(update_kernel, chunk, reach_x, reach_y),...  22.5 us
    another operation x3, local copies, waits for them, and re-layouts, on_device(): jnp.stack([east_vel.reshape(cells), north_vel.reshape(cells)], axis=1)  1.7 us

profile of v3, /device:TPU:13, one launch (start us, length us, event | category | flops | bytes accessed | tf_op | source)
XLA Modules:
  0.0 79.0 jit_solution(2313235928028424460)
XLA Ops:
  0.0 0.7 broadcast_compare_fusion
  0.7 0.8 stack_reshape.12
  1.5 0.8 stack_reshape.13
  2.3 0.7 broadcast_multiply_fusion
  3.0 0.8 %fusion.4 = (f32[3,8,128]{2,1,0:T(8,128)S(1)}, s32[3,128]{1,0:T(4,128)S(1)}, f32[3,8,128]{2,1,0:T(8,128)S(1)}, f32[3,8,128]{2,1,0:T(8,128)S(1)}) fusion(s32[3,8]{1,0:T(4,128)S(1)} %get-tuple-element.9, s32[3,8,128]{2,1,0:T(8,128)} %param.12, pred[3,8]{1,0:T(4,128)(4,1)S(1)} %broadcast_compare_fusion, s32[3,8]{1,0:T(4,128)S(1)} %get-tuple-element.17), kind=kLoop, calls=%fused_computation.14 | loop fusion | flops 137856 | bytes 50904 | tf_op jit(solution)/shard_map/convert_element_type | solution.py:293
  3.8 0.9 %stack.7.line_ref = f32[3,8,1024]{2,1,0:T(8,128)S(1)} concatenate(f32[3,1,1024]{2,1,0:T(1,128)S(1)} %bitcast.19, f32[3,1,1024]{2,1,0:T(1,128)S(1)} %bitcast.17, f32[3,1,1024]{2,1,0:T(1,128)S(1)} %bitcast.15, f32[3,1,1024]{2,1,0:T(1,128)} %bitcast.21, f32[3,1,1024]{2,1,0:T(1,128)} %bitcast.22, f32[3,1,1024]{2,1,0:T(1,128)S(1)} %bitcast.20, f32[3,1,1024]{2,1,0:T(1,128)S(1)} %bitcast.18, ...), dimensions={1} | concatenate | bytes 196608 | tf_op jit(solution)/shard_map/stack | solution.py:293
  4.7 0.1 copy.15
  4.8 0.1 copy.12.speed_ref
  5.0 0.0 copy-start
  5.0 1.0 %copy-done = f32[2,8,32,256]{3,2,1,0:T(8,128)S(1)} copy-done((f32[2,8,32,256]{3,2,1,0:T(8,128)S(1)}, f32[2,8,32,256]{3,2,1,0:T(8,128)}, u32[]{:S(2)}) %copy-start) | copy-done | bytes 524312
  6.0 50.4 %shard_map.82 = (f32[512,256]{1,0:T(8,128)S(1)}, f32[3,4,8,4,16,128]{5,4,3,2,1,0:T(8,128)S(1)}) custom-call(s32[3,8]{1,0:T(4,128)S(1)} %get-tuple-element.18.column_ref, s32[3,8]{1,0:T(4,128)S(1)} %get-tuple-element.10.row_ref, f32[2,8,32,256]{3,2,1,0:T(8,128)S(1)} %copy-done, f32[512,2]{1,0:T(8,128)S(1)} %copy.12.speed_ref, s32[384,1]{1,0:T(8,128)S(1)} %bitcast.13), custom_call_target="tpu_custom_call" | custom-call | tf_op jit(solution)/shard_map/pallas_call | solution.py:162
  56.5 22.5 %shard_map.83 = f32[512,256]{1,0:T(8,128)} custom-call(f32[512,256]{1,0:T(8,128)S(1)} %get-tuple-element.7.state_ref, f32[3,4,8,4,16,128]{5,4,3,2,1,0:T(8,128)S(1)} %get-tuple-element.8.slots_ref, f32[3,1024,256]{2,1,0:T(8,128)} %bitcast.14, f32[3,8,1024]{2,1,0:T(8,128)S(1)} %stack.7.line_ref, f32[8,512]{1,0:T(8,128)S(1)} %stack.8.own_ref), custom_call_target="tpu_custom_call" | custom-call | tf_op jit(solution)/shard_map/pallas_call | solution.py:257
  (5 shorter events, 0.1 us)
Async XLA Ops:
  5.0 1.0 %copy-start = (f32[2,8,32,256]{3,2,1,0:T(8,128)S(1)}, f32[2,8,32,256]{3,2,1,0:T(8,128)}, u32[]{:S(2)}) copy-start(f32[2,8,32,256]{3,2,1,0:T(8,128)} %prior_ref.1) | copy-start | bytes 1572868
